TPU v7x, 32 devices: a whole 2x2x4 slice. The times are simulated.
32 devices in a mesh: row: 2 (over y), col: 16 (over z, x, core).
Axes of the slice: x: 2, y: 2, z: 4, core: 2. Of those that a mesh axis runs over, the one named last changes fastest.
Arguments:
- pair_density: bfloat16 [2048, 4000], P(('row', 'col')), may hold values from -1 to 1
- coulomb: float32 [4000], replicated, may hold values from 0.1 to 10
Outputs:
- kernel: float32 [2048, 16, 128], P('row', 'col')
All inputs are finite; a program needn't handle non-finite values.
Results may differ from a plain program's by a relative error of at most 0.0038.
Values may be sent and summed in bfloat16 or wider, within the bound.
A program may use at most 128 MiB of HBM per device.

v0:
```python
import jax
import jax.numpy as jnp
from jax import lax
from jax.sharding import PartitionSpec as P


def product(first_op, second_op):
    return lax.dot_general(
        first_op, second_op, (((1,), (1,)), ((), ())), preferred_element_type=jnp.float32
    )


def on_device(pair_density, coulomb):
    scaled = (jnp.sqrt(coulomb)[None, :] * pair_density.astype(jnp.float32)).astype(jnp.bfloat16)
    band_pairs = scaled.shape[0]
    col_count = lax.axis_size("col")
    row_count = lax.axis_size("row")
    my_row = lax.axis_index("row")
    my_col = lax.axis_index("col")
    rows_all = lax.all_gather(scaled, "col", axis=0, tiled=True)
    piece = lax.all_gather(scaled, "row", axis=0, tiled=True)
    piece_rows = piece.shape[0]
    last_slot = (jnp.int32(0) + piece_rows - 1) // band_pairs
    computed = lax.cond(
        last_slot >= my_row,
        lambda: product(rows_all, piece),
        lambda: jnp.zeros((rows_all.shape[0], piece_rows), jnp.float32),
    )
    tile_grid = computed.reshape(col_count, band_pairs, row_count, band_pairs)
    row_kpoint = my_row * col_count + jnp.arange(col_count, dtype=jnp.int32)[:, None, None, None]
    col_kpoint = jnp.arange(row_count, dtype=jnp.int32)[None, None, :, None] * col_count + my_col
    upper_keep = (row_kpoint <= col_kpoint).astype(jnp.float32)
    lower_take = (row_kpoint > col_kpoint).astype(jnp.float32)
    own_upper = tile_grid * upper_keep
    received = lax.all_to_all(
        lax.all_to_all(own_upper, "row", split_axis=2, concat_axis=2, tiled=True),
        "col",
        split_axis=0,
        concat_axis=0,
        tiled=True,
    )
    mirrored = jnp.transpose(received, (0, 3, 2, 1))
    kernel = own_upper + lower_take * mirrored
    kernel = kernel.reshape(col_count * band_pairs, row_count * band_pairs)
    return kernel.reshape(col_count * band_pairs, 1, row_count * band_pairs)


def solution(mesh):
    in_specs = (P(("row", "col"), None), P())
    out_specs = P("row", "col", None)
    return jax.shard_map(
        on_device, mesh=mesh, in_specs=in_specs, out_specs=out_specs, check_vma=False
    )
```

profile of v0, /device:TPU:0, one launch (start us, length us, event | category | flops | bytes accessed | tf_op | source)
XLA Modules:
  0.0 139.5 jit_solution(2483025583098075511)
XLA Ops:
  6.5 0.0 all-gather.2.cloned.1.call-start
  6.5 0.7 sqrt.3
  7.3 1.9 %multiply_convert_fusion = bf16[64,4000]{1,0:T(8,128)(2,1)} fusion(bf16[64,4000]{1,0:T(8,128)(2,1)} %param.4, f32[4000]{0:T(1024)S(1)} %sqrt.3), kind=kLoop, calls=%fused_computation.2 | loop fusion | flops 768000 | bytes 1040000 | tf_op jit(solution)/shard_map/convert_element_type | solution.py:14
  9.2 0.0 all-gather.2.cloned.1.call-update
  9.2 0.1 compare_convert_fusion
  9.3 15.8 %all_gather.7 = bf16[128,4000]{1,0:T(8,128)(2,1)S(1)} all-gather(bf16[64,4000]{1,0:T(8,128)(2,1)} %multiply_convert_fusion), channel_id=1, replica_groups=mesh['row'=2,'col'=16] {'row'}, dimensions={0}, use_global_device_ids=true | all-gather | bytes 1536000 | tf_op jit(solution)/shard_map/all_gather | solution.py:21
  25.1 62.0 %all-gather.2.cloned.1.call-done = bf16[1024,4000]{1,0:T(8,128)(2,1)} async-done(((bf16[64,4000]{1,0:T(8,128)(2,1)}), bf16[1024,4000]{1,0:T(8,128)(2,1)}) %all-gather.2.cloned.1.call-update) | async-done | bytes 8192016 | tf_op jit(solution)/shard_map/all_gather | solution.py:20
  87.1 6.9 %conditional.1 = (f32[16,64,2,64]{1,3,0,2:T(8,128)S(1)}) conditional(s32[]{:T(128)} %convert_element_type.25, () %tuple.13, (bf16[1024,4000]{1,0:T(8,128)(2,1)}, bf16[128,4000]{1,0:T(8,128)(2,1)S(1)}) %tuple.14), branch_computations={%region_0.1_spmd, %region_1.2_spmd} | conditional | flops 1048576000 | bytes 11837448 | solution.py:24
  87.1 5.7 %fusion.1 = f32[1024,128]{1,0:T(8,128)S(1)} fusion(bf16[1024,4000]{1,0:T(8,128)(2,1)} %get-tuple-element.13, bf16[128,4000]{1,0:T(8,128)(2,1)S(1)} %get-tuple-element.14), kind=kOutput, calls=%fused_computation.9 | convolution fusion | flops 1048576000 | bytes 9740288 | tf_op jit(solution)/shard_map/cond/branch_1_fun/dot_general | solution.py:8
  92.9 0.6 reshape.85
  93.5 0.5 copy.17
  94.0 0.1 fusion
  94.1 0.7 reshape.87
  94.8 11.1 %all_to_all.10 = f32[2,1,65536]{2,1,0:T(1,128)S(1)} all-to-all(f32[2,1,65536]{2,1,0:T(1,128)S(1)} %reshape.87), channel_id=1, replica_groups=mesh['row'=2,'col'=16] {'row'}, dimensions={0} | all-to-all | bytes 1048576 | tf_op jit(solution)/shard_map/all_to_all | solution.py:36
  105.9 0.5 broadcast.68
  106.4 2.3 %reduce = f32[2,65536]{1,0:T(2,128)S(1)} reduce(f32[2,1,65536]{2,1,0:T(1,128)S(1)} %all_to_all.10, f32[]{:T(128)} %broadcast.68), dimensions={1}, to_apply=%all_to_all.6.reduce_sub_computation | reduce | bytes 1048580 | tf_op jit(solution)/shard_map/all_to_all | solution.py:36
  108.7 0.6 reshape.88
  109.4 0.3 copy.11
  109.7 0.7 reshape.89
  110.4 17.3 %all_to_all.11 = f32[16,1,8192]{2,1,0:T(1,128)S(1)} all-to-all(f32[16,1,8192]{2,1,0:T(1,128)S(1)} %reshape.89), channel_id=1, replica_groups=mesh['row'=2,'col'=16] {'col'}, dimensions={0} | all-to-all | bytes 1048576 | tf_op jit(solution)/shard_map/all_to_all | solution.py:35
  127.7 1.9 %reduce.1 = f32[16,8192]{1,0:T(8,128)S(1)} reduce(f32[16,1,8192]{2,1,0:T(1,128)S(1)} %all_to_all.11, f32[]{:T(128)} %broadcast.68), dimensions={1}, to_apply=%all_to_all.7.reduce_sub_computation | reduce | bytes 1048580 | tf_op jit(solution)/shard_map/all_to_all | solution.py:35
  129.6 0.4 reshape.90
  130.0 0.2 bitcast_add_fusion
  130.2 0.6 copy.15
  130.8 1.9 %reshape.86 = f32[1024,1,128]{2,1,0:T(1,128)} reshape(f32[16,64,2,64]{3,2,1,0:T(2,128)S(1)} %copy.15) | data formatting | bytes 1048576 | tf_op jit(solution)/shard_map/reshape;reshape | solution.py:45
  (2 shorter events, 0.0 us)
Async XLA Ops:
  6.5 80.6 %all-gather.2.cloned.1.call-start = ((), (), s32[]{:S(2)}) async-start(), calls=%async_computation.2 | async-start | bytes 8912896 | tf_op jit(solution)/shard_map/all_gather | solution.py:20
Sparse Core Ops, SparseCore 0:
  9.5 77.5 all-gather.1
where the time goes:
time: 140 us
  waiting for transfers between devices  62 us (44%)
  blocking collectives  44.2 us (32%)
  between operations  13.5 us (10%)
  local copies, waits for them, and re-layouts  7.59 us (5%)
  other arithmetic  6.51 us (5%)
  matrix products  5.71 us (4%)
    all_gather x1, waiting for transfers between devices, on_device(): rows_all = lax.all_gather(scaled, 'col', axis=0, tiled=True)  62 us
    all_to_all x1, blocking collectives, on_device(): lax.all_to_all(lax.all_to_all(own_upper, 'row', split_axis=2, concat_axis...  17.3 us
    all_gather x1, blocking collectives, on_device(): piece = lax.all_gather(scaled, 'row', axis=0, tiled=True)  15.8 us
    all_to_all x1, blocking collectives, on_device(): lax.all_to_all(own_upper, 'row', split_axis=2, concat_axis=2, tiled=True)  11.1 us
    dot_general x1, matrix products, product(): lax.dot_general(first_op, second_op, (((1,), (1,)), ((), ())), preferred_...  5.71 us
  transfers between devices with their start and end apart: 1, of which 1 were waited for; matrix products, arithmetic and copies ran while one was open for 0% of the time, Pallas kernels for 0%

commit v1 on v0

v1 whole, which is shorter than its diff:
```python
import functools

import jax
import jax.numpy as jnp
from jax import lax
from jax.experimental import pallas as pl
from jax.experimental.pallas import tpu as pltpu
from jax.sharding import PartitionSpec as P

UP, DOWN, SIDE, TWIN = range(4)
PARTS = 4


def body(rows, cols, pair_ref, root_ref, out_ref, held, piece, send_sem, recv_sem, row_send, row_recv):
    band = pair_ref.shape[0]
    part = band // PARTS
    line = cols // 4
    my_row = lax.axis_index("row")
    me = lax.axis_index("col")
    core = lax.rem(me, 2)
    x = lax.rem(me // 2, 2)
    z = me // 4

    def col_of(zz, xx, cc):
        return (zz * 2 + xx) * 2 + cc

    def device(way):
        if way == UP:
            target = col_of(z + 1, x, core)
        elif way == DOWN:
            target = col_of(z - 1, x, core)
        elif way == SIDE:
            target = col_of(z, 1 - x, core)
        else:
            target = col_of(z, x, 1 - core)
        return (my_row, target)

    def window(slot, k):
        return pl.ds(pl.multiple_of(slot * band + k * part, part), part)

    def copy(way, slot, k):
        return pltpu.make_async_remote_copy(
            src_ref=held.at[window(slot, k)],
            dst_ref=held.at[window(slot, k)],
            send_sem=send_sem.at[way, slot, k],
            recv_sem=recv_sem.at[slot, k],
            device_id=device(way),
            device_id_type=pl.DeviceIdType.MESH,
        )

    def arrive(slot, k):
        copy(SIDE, slot, k).wait_recv()

    def row_copy(step, k):
        target = lax.rem(my_row + step, rows)
        return pltpu.make_async_remote_copy(
            src_ref=held.at[window(me, k)],
            dst_ref=piece.at[window(my_row, k)],
            send_sem=row_send.at[target, k],
            recv_sem=row_recv.at[my_row, k],
            device_id=(target, me),
            device_id_type=pl.DeviceIdType.MESH,
        )

    def row_arrive(step, k):
        source = lax.rem(my_row + step, rows)
        pltpu.make_async_remote_copy(
            src_ref=piece.at[window(source, k)],
            dst_ref=piece.at[window(source, k)],
            send_sem=row_send.at[source, k],
            recv_sem=row_recv.at[source, k],
            device_id=(source, me),
            device_id_type=pl.DeviceIdType.MESH,
        ).wait_recv()

    has_up = z < line - 1
    has_down = z > 0

    barrier = pltpu.get_barrier_semaphore()

    def greet(target):
        pl.semaphore_signal(barrier, inc=1, device_id=target, device_id_type=pl.DeviceIdType.MESH)

    greet(device(SIDE))
    greet(device(TWIN))
    for step in range(1, rows):
        greet((lax.rem(my_row + step, rows), me))

    @pl.when(has_up)
    def _():
        greet(device(UP))

    @pl.when(has_down)
    def _():
        greet(device(DOWN))

    for k in range(PARTS):
        here = pl.ds(k * part, part)
        value = (root_ref[...] * pair_ref[here].astype(jnp.float32)).astype(jnp.bfloat16)
        held[window(me, k)] = value
        piece[window(my_row, k)] = value
        if k == 0:
            ends = (z == 0).astype(jnp.int32) + (z == line - 1).astype(jnp.int32)
            pl.semaphore_wait(barrier, 3 + rows - ends)

        @pl.when(has_up)
        def _():
            copy(UP, me, k).start()

        @pl.when(has_down)
        def _():
            copy(DOWN, me, k).start()

        copy(SIDE, me, k).start()
        copy(TWIN, me, k).start()
        for step in range(1, rows):
            row_copy(step, k).start()

    def forward(d, _):
        def each(k, _):
            @pl.when(z - d >= 0)
            def _():
                slot = col_of(z - d, x, core)
                arrive(slot, k)

                @pl.when(has_up)
                def _():
                    copy(UP, slot, k).start()

                copy(SIDE, slot, k).start()
                copy(TWIN, slot, k).start()

            @pl.when(z + d < line)
            def _():
                slot = col_of(z + d, x, core)
                arrive(slot, k)

                @pl.when(has_down)
                def _():
                    copy(DOWN, slot, k).start()

                copy(SIDE, slot, k).start()
                copy(TWIN, slot, k).start()

            return 0

        return lax.fori_loop(0, PARTS, each, 0)

    lax.fori_loop(1, line, forward, 0)

    def row_wait(k, _):
        for step in range(1, rows):
            row_arrive(step, k)
        return 0

    lax.fori_loop(0, PARTS, row_wait, 0)

    def product(zz, xx):
        def each(k, _):
            arrive(col_of(zz, xx, 1 - core), k)
            return 0

        lax.fori_loop(0, PARTS, each, 0)
        start = pl.multiple_of(col_of(zz, xx, 0) * band, 2 * band)
        out_ref[pl.ds(start, 2 * band)] = lax.dot_general(
            held[pl.ds(start, 2 * band)],
            piece[...],
            (((1,), (1,)), ((), ())),
            preferred_element_type=jnp.float32,
        )

    def settle(d, _):
        def one(zz):
            def each(k, _):
                slot = col_of(zz, 1 - x, core)
                arrive(slot, k)
                copy(TWIN, slot, k).start()
                return 0

            product(zz, x)
            lax.fori_loop(0, PARTS, each, 0)
            product(zz, 1 - x)

        def both(sign, _):
            zz = z + sign * d

            @pl.when((zz >= 0) & (zz < line) & ((d > 0) | (sign > 0)))
            def _():
                one(zz)

            return 0

        return lax.fori_loop(0, 2, lambda s, c: both(2 * s - 1, c), 0)

    lax.fori_loop(0, line, settle, 0)

    def drain(zz, _):
        def each(k, _):
            mine = col_of(zz, x, core)
            copy(SIDE, mine, k).wait_send()
            copy(TWIN, mine, k).wait_send()
            copy(TWIN, col_of(zz, 1 - x, core), k).wait_send()

            @pl.when(has_up & (zz <= z))
            def _():
                copy(UP, mine, k).wait_send()

            @pl.when(has_down & (zz >= z))
            def _():
                copy(DOWN, mine, k).wait_send()

            return 0

        return lax.fori_loop(0, PARTS, each, 0)

    lax.fori_loop(0, line, drain, 0)

    def row_drain(k, _):
        for step in range(1, rows):
            row_copy(step, k).wait_send()
        return 0

    lax.fori_loop(0, PARTS, row_drain, 0)


def on_device(rows, cols, pair_density, coulomb):
    band, comps = pair_density.shape
    root = jnp.sqrt(coulomb)[None, :]
    vmem = pl.BlockSpec(memory_space=pltpu.VMEM)
    kernel = pl.pallas_call(
        functools.partial(body, rows, cols),
        out_shape=jax.ShapeDtypeStruct((cols * band, rows * band), jnp.float32),
        in_specs=[vmem, vmem],
        out_specs=vmem,
        scratch_shapes=[
            pltpu.VMEM((cols * band, comps), jnp.bfloat16),
            pltpu.VMEM((rows * band, comps), jnp.bfloat16),
            pltpu.SemaphoreType.DMA((4, cols, PARTS)),
            pltpu.SemaphoreType.DMA((cols, PARTS)),
            pltpu.SemaphoreType.DMA((rows, PARTS)),
            pltpu.SemaphoreType.DMA((rows, PARTS)),
        ],
        compiler_params=pltpu.CompilerParams(
            collective_id=0, has_side_effects=True, vmem_limit_bytes=48 * 1024 * 1024
        ),
        cost_estimate=pl.CostEstimate(
            flops=2 * cols * rows * band * band * comps,
            bytes_accessed=2 * band * comps + 4 * cols * rows * band * band,
            transcendentals=0,
        ),
    )(pair_density, root)
    return kernel.reshape(cols * band, 1, rows * band)


def solution(mesh):
    rows, cols = mesh.shape["row"], mesh.shape["col"]
    in_specs = (P(("row", "col"), None), P())
    out_specs = P("row", "col", None)
    return jax.shard_map(
        functools.partial(on_device, rows, cols),
        mesh=mesh,
        in_specs=in_specs,
        out_specs=out_specs,
        check_vma=False,
    )
```

time: 140 us -> 57.7 us (0.41)
  waiting for transfers between devices: 62 us -> 0 us
  Pallas kernels: 0 us -> 54.5 us
  blocking collectives: 44.2 us -> 0 us
  between operations: 13.5 us -> 0.01 us
  other arithmetic: 6.51 us -> 0 us
  matrix products: 5.71 us -> 0 us
  local copies, waits for them, and re-layouts: 7.59 us -> 2.56 us
    all_gather x1 -> x0, waiting for transfers between devices: 62 us -> none  [on_device(): rows_all = lax.all_gather(scaled, 'col', axis=0, tiled=True)]
    pallas_call x0 -> x1, Pallas kernels: none -> 54.5 us  [on_device(): pl.pallas_call(functools.partial(body, rows, cols), out_shape=jax.ShapeDt...]
    all_to_all x2 -> x0, blocking collectives: 28.4 us -> none  [the longest x1 17.3 us: on_device(): lax.all_to_all(lax.all_to_all(own_upper, 'row', split_axis=2, concat_axis...]
    all_gather x1 -> x0, blocking collectives: 15.8 us -> none  [on_device(): piece = lax.all_gather(scaled, 'row', axis=0, tiled=True)]
    dot_general x1 -> x0, matrix products: 5.71 us -> none  [product(): lax.dot_general(first_op, second_op, (((1,), (1,)), ((), ())), preferred_...]
    all_to_all x2 -> x0, other arithmetic: 4.19 us -> none  [the longest x1 2.3 us: on_device(): lax.all_to_all(own_upper, 'row', split_axis=2, concat_axis=2, tiled=True)]
    another operation x2 -> x0, local copies, waits for them, and re-layouts: 2.52 us -> none  [on_device(): return kernel.reshape(col_count * band_pairs, 1, row_count * band_pairs)]
    convert_element_type x2 -> x0, other arithmetic: 2 us -> none  [the longest x1 1.92 us: on_device(): (jnp.sqrt(coulomb)[None, :] * pair_density.astype(jnp.float32)).astype(jn...]
  transfers between devices with their start and end apart: 1 -> 0, of which waited for: 1 -> 0; matrix products, arithmetic and copies ran while one was open for 0% -> 0% of each run, Pallas kernels for 0% -> 0%
where the time goes in v1:
time: 57.7 us; the launch traced here: 57.1 us
  Pallas kernels  54.5 us (94%)
  local copies, waits for them, and re-layouts  2.56 us (4%)
    pallas_call x1, Pallas kernels, on_device(): pl.pallas_call(functools.partial(body, rows, cols), out_shape=jax.ShapeDt...  54.5 us
    unnamed x3, local copies, waits for them, and re-layouts  1.84 us

profile of v1, /device:TPU:0, one launch (start us, length us, event | category | flops | bytes accessed | tf_op | source)
XLA Modules:
  0.0 57.1 jit_solution(13118258497003884607)
XLA Ops:
  0.0 0.7 %sqrt.3 = f32[4000]{0:T(1024)S(1)} sqrt(f32[4000]{0:T(1024)} %param.3) | non-fusion elementwise | bytes 32000 | tf_op jit(solution)/shard_map/sqrt | solution.py:228
  0.7 0.0 copy-start
  0.7 1.0 %copy-done = bf16[64,4000]{1,0:T(8,128)(2,1)S(1)} copy-done((bf16[64,4000]{1,0:T(8,128)(2,1)S(1)}, bf16[64,4000]{1,0:T(8,128)(2,1)}, u32[]{:S(2)}) %copy-start) | copy-done | bytes 512024
  1.8 54.5 %shard_map.28 = f32[1024,128]{1,0:T(8,128)S(1)} custom-call(bf16[64,4000]{1,0:T(8,128)(2,1)S(1)} %copy-done, f32[1,4000]{1,0:T(1,128)S(1)} %bitcast.5), custom_call_target="tpu_custom_call" | custom-call | flops 1048576000 | bytes 1036288 | tf_op jit(solution)/shard_map/pallas_call | solution.py:230
  56.3 0.8 %copy.5 = f32[1024,1,128]{2,1,0:T(1,128)} copy(f32[1024,1,128]{2,1,0:T(1,128)S(1)} %bitcast.4) | data formatting | bytes 1048576
Async XLA Ops:
  0.7 1.0 %copy-start = (bf16[64,4000]{1,0:T(8,128)(2,1)S(1)}, bf16[64,4000]{1,0:T(8,128)(2,1)}, u32[]{:S(2)}) copy-start(bf16[64,4000]{1,0:T(8,128)(2,1)} %pair_ref.1) | copy-start | bytes 1536004

commit v2 on v1

v2 whole, which is shorter than its diff:
```python
import functools

import jax
import jax.numpy as jnp
from jax import lax
from jax.experimental import pallas as pl
from jax.experimental.pallas import tpu as pltpu
from jax.sharding import PartitionSpec as P

UP, DOWN, SIDE, TWIN = range(4)
PARTS = 4
SWAPPED = 2


def body(rows, cols, pair_ref, weight_ref, out_ref, held, piece, lent, *sems):
    send_sem, recv_sem, row_send, row_recv, lent_send, lent_recv = sems
    band = pair_ref.shape[0]
    part = band // PARTS
    line = cols // 4
    my_row = lax.axis_index("row")
    me = lax.axis_index("col")
    core = lax.rem(me, 2)
    x = lax.rem(me // 2, 2)
    z = me // 4

    def col_of(zz, xx, cc):
        return (zz * 2 + xx) * 2 + cc

    def device(way):
        if way == UP:
            target = col_of(z + 1, x, core)
        elif way == DOWN:
            target = col_of(z - 1, x, core)
        elif way == SIDE:
            target = col_of(z, 1 - x, core)
        else:
            target = col_of(z, x, 1 - core)
        return (my_row, target)

    def window(slot, k):
        return pl.ds(pl.multiple_of(slot * band + k * part, part), part)

    def copy(way, slot, k):
        return pltpu.make_async_remote_copy(
            src_ref=held.at[window(slot, k)],
            dst_ref=held.at[window(slot, k)],
            send_sem=send_sem.at[way, slot, k],
            recv_sem=recv_sem.at[slot, k],
            device_id=device(way),
            device_id_type=pl.DeviceIdType.MESH,
        )

    def arrive(slot, k):
        copy(SIDE, slot, k).wait_recv()

    def row_copy(step, ward, k):
        target = lax.rem(my_row + step, rows)
        return pltpu.make_async_remote_copy(
            src_ref=held.at[window(ward_slot if ward else me, k)],
            dst_ref=piece.at[window(ward * rows + my_row, k)],
            send_sem=row_send.at[ward, target, k],
            recv_sem=row_recv.at[ward, my_row, k],
            device_id=(target, me),
            device_id_type=pl.DeviceIdType.MESH,
        )

    def row_arrive(step, ward, k):
        source = lax.rem(my_row + step, rows)
        pltpu.make_async_remote_copy(
            src_ref=piece.at[window(ward * rows + source, k)],
            dst_ref=piece.at[window(ward * rows + source, k)],
            send_sem=row_send.at[ward, source, k],
            recv_sem=row_recv.at[ward, source, k],
            device_id=(source, me),
            device_id_type=pl.DeviceIdType.MESH,
        ).wait_recv()

    def chip_rows(zz, xx):
        return pl.ds(pl.multiple_of(col_of(zz, xx, 0) * band, 2 * band), 2 * band)

    def lent_copy(zz, xx):
        return pltpu.make_async_remote_copy(
            src_ref=lent.at[chip_rows(zz, xx)],
            dst_ref=lent.at[chip_rows(zz, xx)],
            send_sem=lent_send.at[zz, xx],
            recv_sem=lent_recv.at[zz, xx],
            device_id=(my_row, ward_slot),
            device_id_type=pl.DeviceIdType.MESH,
        )

    end = (z == 0) | (z == line - 1)
    inner = jnp.logical_not(end)
    helper = (z == 1) | (z == line - 2)
    ward_z = jnp.where(z == 1, 0, jnp.where(end, jnp.where(z == 0, 1, line - 2), line - 1))
    ward_slot = col_of(ward_z, x, core)
    to_up = z < line - 2
    to_down = z > 1

    def goes_side(zz, k):
        far = (zz < z - 1) | (zz > z + 1)
        middle = (zz > 0) & (zz < line - 1) & (k >= SWAPPED)
        return (zz == z) | (inner & (far | middle))

    has_up = z < line - 1
    has_down = z > 0

    barrier = pltpu.get_barrier_semaphore()

    def greet(target):
        pl.semaphore_signal(barrier, inc=1, device_id=target, device_id_type=pl.DeviceIdType.MESH)

    greet(device(SIDE))
    greet(device(TWIN))
    for step in range(1, rows):
        greet((lax.rem(my_row + step, rows), me))

    @pl.when(has_up)
    def _():
        greet(device(UP))

    @pl.when(has_down)
    def _():
        greet(device(DOWN))

    root = jnp.sqrt(weight_ref[...])
    for k in range(PARTS):
        here = pl.ds(k * part, part)
        value = (root * pair_ref[here].astype(jnp.float32)).astype(jnp.bfloat16)
        held[window(me, k)] = value

        @pl.when(inner)
        def _():
            piece[window(my_row, k)] = value

        if k == 0:
            ends = (z == 0).astype(jnp.int32) + (z == line - 1).astype(jnp.int32)
            pl.semaphore_wait(barrier, 3 + rows - ends)

        @pl.when(to_up)
        def _():
            copy(UP, me, k).start()

        @pl.when(to_down)
        def _():
            copy(DOWN, me, k).start()

        copy(SIDE, me, k).start()

        @pl.when(inner)
        def _():
            copy(TWIN, me, k).start()
            for step in range(1, rows):
                row_copy(step, 0, k).start()

    def relay(zz, way, onward):
        def each(k, _):
            slot = col_of(zz, x, core)
            arrive(slot, k)

            @pl.when(onward)
            def _():
                copy(way, slot, k).start()

            @pl.when(goes_side(zz, k))
            def _():
                copy(SIDE, slot, k).start()

            copy(TWIN, slot, k).start()

            @pl.when(helper & (slot == ward_slot))
            def _():
                piece[window(rows + my_row, k)] = held[window(slot, k)]
                for step in range(1, rows):
                    row_copy(step, 1, k).start()

            return 0

        lax.fori_loop(0, PARTS, each, 0)

    def forward(d, _):
        @pl.when(inner & (z - d >= 0))
        def _():
            relay(z - d, UP, to_up)

        @pl.when(inner & (z + d < line))
        def _():
            relay(z + d, DOWN, to_down)

        return 0

    lax.fori_loop(1, line, forward, 0)

    beside = col_of(z, 1 - x, core)

    def beside_each(k, _):
        arrive(beside, k)

        @pl.when(to_up & (end | (k < SWAPPED)))
        def _():
            copy(UP, beside, k).start()

        @pl.when(to_down & (end | (k < SWAPPED)))
        def _():
            copy(DOWN, beside, k).start()

        @pl.when(inner)
        def _():
            copy(TWIN, beside, k).start()

        return 0

    lax.fori_loop(0, PARTS, beside_each, 0)

    def row_wait(ward):
        def each(k, _):
            for step in range(1, rows):
                row_arrive(step, ward, k)
            return 0

        lax.fori_loop(0, PARTS, each, 0)

    @pl.when(inner)
    def _():
        row_wait(0)

    @pl.when(helper)
    def _():
        row_wait(1)

    def multiply(start, wide):
        return lax.dot_general(
            held[start], piece[: wide * band], (((1,), (1,)), ((), ())), preferred_element_type=jnp.float32
        )

    def product(zz, xx):
        def each(k, _):
            arrive(col_of(zz, xx, 1 - core), k)
            return 0

        lax.fori_loop(0, PARTS, each, 0)
        start = chip_rows(zz, xx)

        @pl.when(helper)
        def _():
            both = multiply(start, 2 * rows)
            lent[start] = both[:, rows * band :]
            lent_copy(zz, xx).start()
            out_ref[start] = both[:, : rows * band]

        if line > 4:

            @pl.when(jnp.logical_not(helper))
            def _():
                out_ref[start] = multiply(start, rows)

    def settle(t, _):
        d = t // 2
        zz = jnp.where(lax.rem(t, 2) == 0, z - d, z + d)

        @pl.when((zz >= 0) & (zz < line) & (t != 0))
        def _():
            def each(k, _):
                slot = col_of(zz, 1 - x, core)
                arrive(slot, k)
                copy(TWIN, slot, k).start()
                return 0

            product(zz, x)

            @pl.when(d > 0)
            def _():
                lax.fori_loop(0, PARTS, each, 0)

            product(zz, 1 - x)

        return 0

    @pl.when(inner)
    def _():
        lax.fori_loop(1, 2 * line, settle, 0)

    @pl.when(end)
    def _():
        def take(t, _):
            d = t // 2
            zz = jnp.where(z == 0, lax.rem(d + 1, line), lax.rem(2 * line - 2 - d, line))
            xx = lax.rem(x + t, 2)
            lent_copy(zz, xx).wait_recv()
            out_ref[chip_rows(zz, xx)] = lent[chip_rows(zz, xx)]
            return 0

        lax.fori_loop(0, 2 * line, take, 0)

    def drain(zz, _):
        def each(k, _):
            mine = col_of(zz, x, core)

            @pl.when(goes_side(zz, k))
            def _():
                copy(SIDE, mine, k).wait_send()

            @pl.when(inner)
            def _():
                copy(TWIN, mine, k).wait_send()
                copy(TWIN, col_of(zz, 1 - x, core), k).wait_send()

            @pl.when(to_up & (zz <= z))
            def _():
                copy(UP, mine, k).wait_send()

            @pl.when(to_down & (zz >= z))
            def _():
                copy(DOWN, mine, k).wait_send()

            return 0

        lax.fori_loop(0, PARTS, each, 0)

        @pl.when(helper)
        def _():
            for xx in range(2):
                lent_copy(zz, xx).wait_send()

        return 0

    lax.fori_loop(0, line, drain, 0)

    def last(k, _):
        @pl.when(to_up & (end | (k < SWAPPED)))
        def _():
            copy(UP, beside, k).wait_send()

        @pl.when(to_down & (end | (k < SWAPPED)))
        def _():
            copy(DOWN, beside, k).wait_send()

        for step in range(1, rows):

            @pl.when(inner)
            def _():
                row_copy(step, 0, k).wait_send()

            @pl.when(helper)
            def _():
                row_copy(step, 1, k).wait_send()

        return 0

    lax.fori_loop(0, PARTS, last, 0)


def on_device(rows, cols, pair_density, coulomb):
    band, comps = pair_density.shape
    weight = coulomb[None, :]
    vmem = pl.BlockSpec(memory_space=pltpu.VMEM)
    kernel = pl.pallas_call(
        functools.partial(body, rows, cols),
        out_shape=jax.ShapeDtypeStruct((cols * band, rows * band), jnp.float32),
        in_specs=[vmem, vmem],
        out_specs=vmem,
        scratch_shapes=[
            pltpu.VMEM((cols * band, comps), jnp.bfloat16),
            pltpu.VMEM((2 * rows * band, comps), jnp.bfloat16),
            pltpu.VMEM((cols * band, rows * band), jnp.float32),
            pltpu.SemaphoreType.DMA((4, cols, PARTS)),
            pltpu.SemaphoreType.DMA((cols, PARTS)),
            pltpu.SemaphoreType.DMA((2, rows, PARTS)),
            pltpu.SemaphoreType.DMA((2, rows, PARTS)),
            pltpu.SemaphoreType.DMA((cols // 4, 2)),
            pltpu.SemaphoreType.DMA((cols // 4, 2)),
        ],
        compiler_params=pltpu.CompilerParams(
            collective_id=0, has_side_effects=True, vmem_limit_bytes=48 * 1024 * 1024
        ),
        cost_estimate=pl.CostEstimate(
            flops=2 * cols * rows * band * band * comps,
            bytes_accessed=2 * band * comps + 4 * cols * rows * band * band,
            transcendentals=0,
        ),
    )(pair_density, weight)
    return kernel.reshape(cols * band, 1, rows * band)


def solution(mesh):
    rows, cols = mesh.shape["row"], mesh.shape["col"]
    in_specs = (P(("row", "col"), None), P())
    out_specs = P("row", "col", None)
    return jax.shard_map(
        functools.partial(on_device, rows, cols),
        mesh=mesh,
        in_specs=in_specs,
        out_specs=out_specs,
        check_vma=False,
    )
```

time: 57.7 us -> 51.1 us (0.89)
  Pallas kernels: 54.5 us -> 48.3 us
    pallas_call x1, Pallas kernels: 54.5 us -> 48.3 us  [on_device(): pl.pallas_call(functools.partial(body, rows, cols), out_shape=jax.ShapeDt...]
    sqrt x1 -> x0, local copies, waits for them, and re-layouts: 0.72 us -> none  [on_device(): root = jnp.sqrt(coulomb)[None, :]]
    unnamed x3 -> x5, local copies, waits for them, and re-layouts: 1.84 us -> 2.55 us
where the time goes in v2:
time: 51.1 us; the launch traced here: 50.9 us
  Pallas kernels  48.3 us (95%)
  local copies, waits for them, and re-layouts  2.55 us (5%)
    pallas_call x1, Pallas kernels, on_device(): pl.pallas_call(functools.partial(body, rows, cols), out_shape=jax.ShapeDt...  48.3 us
    unnamed x5, local copies, waits for them, and re-layouts  2.55 us

profile of v2, /device:TPU:0, one launch (start us, length us, event | category | flops | bytes accessed | tf_op | source)
XLA Modules:
  0.0 50.9 jit_solution(14581630023232947845)
XLA Ops:
  0.0 0.0 copy-start
  0.0 1.0 %copy-done = bf16[64,4000]{1,0:T(8,128)(2,1)S(1)} copy-done((bf16[64,4000]{1,0:T(8,128)(2,1)S(1)}, bf16[64,4000]{1,0:T(8,128)(2,1)}, u32[]{:S(2)}) %copy-start) | copy-done | bytes 512024
  1.0 0.0 copy-start.1
  1.0 0.7 %copy-done.1 = f32[4000]{0:T(1024)S(1)} copy-done((f32[4000]{0:T(1024)S(1)}, f32[4000]{0:T(1024)}, u32[]{:S(2)}) %copy-start.1) | copy-done | bytes 16024
  1.8 48.3 %shard_map.28 = f32[1024,128]{1,0:T(8,128)S(1)} custom-call(bf16[64,4000]{1,0:T(8,128)(2,1)S(1)} %copy-done, f32[1,4000]{1,0:T(1,128)S(1)} %bitcast.5), custom_call_target="tpu_custom_call" | custom-call | flops 1048576000 | bytes 1036288 | tf_op jit(solution)/shard_map/pallas_call | solution.py:356
  50.1 0.8 %copy.5 = f32[1024,1,128]{2,1,0:T(1,128)} copy(f32[1024,1,128]{2,1,0:T(1,128)S(1)} %bitcast.4) | data formatting | bytes 1048576
Async XLA Ops:
  0.0 1.0 %copy-start = (bf16[64,4000]{1,0:T(8,128)(2,1)S(1)}, bf16[64,4000]{1,0:T(8,128)(2,1)}, u32[]{:S(2)}) copy-start(bf16[64,4000]{1,0:T(8,128)(2,1)} %pair_ref.1) | copy-start | bytes 1536004
  1.0 0.7 %copy-start.1 = (f32[4000]{0:T(1024)S(1)}, f32[4000]{0:T(1024)}, u32[]{:S(2)}) copy-start(f32[4000]{0:T(1024)} %param.3) | copy-start | bytes 48004

commit v3 on v2

--- a/solution.py
+++ b/solution.py
@@ -10,6 +10,7 @@
 UP, DOWN, SIDE, TWIN = range(4)
 PARTS = 4
 SWAPPED = 2
+LAG = 2
 
 
 def body(rows, cols, pair_ref, weight_ref, out_ref, held, piece, lent, *sems):
@@ -132,84 +133,101 @@
         def _():
             piece[window(my_row, k)] = value
 
-        if k == 0:
-            ends = (z == 0).astype(jnp.int32) + (z == line - 1).astype(jnp.int32)
-            pl.semaphore_wait(barrier, 3 + rows - ends)
-
-        @pl.when(to_up)
-        def _():
-            copy(UP, me, k).start()
-
-        @pl.when(to_down)
-        def _():
-            copy(DOWN, me, k).start()
-
-        copy(SIDE, me, k).start()
-
-        @pl.when(inner)
-        def _():
-            copy(TWIN, me, k).start()
-            for step in range(1, rows):
-                row_copy(step, 0, k).start()
-
-    def relay(zz, way, onward):
-        def each(k, _):
+    ends = (z == 0).astype(jnp.int32) + (z == line - 1).astype(jnp.int32)
+    pl.semaphore_wait(barrier, 3 + rows - ends)
+    beside = col_of(z, 1 - x, core)
+
+    def act(begin, way, slot, k):
+        if begin:
+            copy(way, slot, k).start()
+        else:
+            copy(way, slot, k).wait_send()
+
+    def tick(t, begin):
+        d, k = t // PARTS, lax.rem(t, PARTS)
+        low, high = z - d, z + d
+
+        @pl.when(to_up & (low >= 0) & (inner | (d == 0)))
+        def _():
+            act(begin, UP, col_of(low, x, core), k)
+
+        @pl.when(to_down & (high < line) & (inner | (d == 0)))
+        def _():
+            act(begin, DOWN, col_of(high, x, core), k)
+
+        @pl.when(d == 0)
+        def _():
+            act(begin, SIDE, me, k)
+
+            if begin:
+
+                @pl.when(inner)
+                def _():
+                    copy(TWIN, me, k).start()
+                    for step in range(1, rows):
+                        row_copy(step, 0, k).start()
+
+        if begin:
+
+            @pl.when((t >= LAG) & (t < PARTS + LAG))
+            def _():
+                arrive(beside, t - LAG)
+
+                @pl.when(inner)
+                def _():
+                    copy(TWIN, beside, t - LAG).start()
+
+        swap = jnp.where(end, d == 1, (d == line - 2) & (k < SWAPPED))
+
+        @pl.when(to_up & swap)
+        def _():
+            act(begin, UP, beside, k)
+
+        @pl.when(to_down & swap)
+        def _():
+            act(begin, DOWN, beside, k)
+
+        ahead = (t + SWAPPED) // PARTS
+        part_ahead = lax.rem(t + SWAPPED, PARTS)
+
+        def relay(zz):
             slot = col_of(zz, x, core)
-            arrive(slot, k)
-
-            @pl.when(onward)
-            def _():
-                copy(way, slot, k).start()
-
-            @pl.when(goes_side(zz, k))
-            def _():
-                copy(SIDE, slot, k).start()
-
-            copy(TWIN, slot, k).start()
-
-            @pl.when(helper & (slot == ward_slot))
-            def _():
-                piece[window(rows + my_row, k)] = held[window(slot, k)]
-                for step in range(1, rows):
-                    row_copy(step, 1, k).start()
-
-            return 0
-
-        lax.fori_loop(0, PARTS, each, 0)
-
-    def forward(d, _):
-        @pl.when(inner & (z - d >= 0))
-        def _():
-            relay(z - d, UP, to_up)
-
-        @pl.when(inner & (z + d < line))
-        def _():
-            relay(z + d, DOWN, to_down)
+            if begin:
+                arrive(slot, part_ahead)
+                copy(TWIN, slot, part_ahead).start()
+
+                @pl.when(helper & (slot == ward_slot))
+                def _():
+                    piece[window(rows + my_row, part_ahead)] = held[window(slot, part_ahead)]
+                    for step in range(1, rows):
+                        row_copy(step, 1, part_ahead).start()
+
+            @pl.when(goes_side(zz, part_ahead))
+            def _():
+                act(begin, SIDE, slot, part_ahead)
+
+        @pl.when(inner & (ahead > 0) & (z - ahead >= 0))
+        def _():
+            relay(z - ahead)
+
+        @pl.when(inner & (ahead > 0) & (z + ahead < line))
+        def _():
+            relay(z + ahead)
+
+    ticks = PARTS * (line - 2) + SWAPPED
+
+    def advance(t, _):
+        @pl.when(t >= LAG)
+        def _():
+            tick(t - LAG, False)
+
+        @pl.when(t < ticks)
+        def _():
+            tick(t, True)
 
         return 0
 
-    lax.fori_loop(1, line, forward, 0)
-
-    beside = col_of(z, 1 - x, core)
-
-    def beside_each(k, _):
-        arrive(beside, k)
-
-        @pl.when(to_up & (end | (k < SWAPPED)))
-        def _():
-            copy(UP, beside, k).start()
-
-        @pl.when(to_down & (end | (k < SWAPPED)))
-        def _():
-            copy(DOWN, beside, k).start()
-
-        @pl.when(inner)
-        def _():
-            copy(TWIN, beside, k).start()
-
-        return 0
-
-    lax.fori_loop(0, PARTS, beside_each, 0)
+    lax.fori_loop(0, ticks, advance, 0)
 
     def row_wait(ward):
         def each(k, _):
@@ -291,49 +309,28 @@
 
         lax.fori_loop(0, 2 * line, take, 0)
 
-    def drain(zz, _):
-        def each(k, _):
-            mine = col_of(zz, x, core)
-
-            @pl.when(goes_side(zz, k))
-            def _():
-                copy(SIDE, mine, k).wait_send()
-
-            @pl.when(inner)
-            def _():
-                copy(TWIN, mine, k).wait_send()
-                copy(TWIN, col_of(zz, 1 - x, core), k).wait_send()
-
-            @pl.when(to_up & (zz <= z))
-            def _():
-                copy(UP, mine, k).wait_send()
-
-            @pl.when(to_down & (zz >= z))
-            def _():
-                copy(DOWN, mine, k).wait_send()
+    lax.fori_loop(ticks, ticks + LAG, advance, 0)
+
+    @pl.when(inner)
+    def _():
+        def drain(zz, _):
+            def each(k, _):
+                for xx in range(2):
+                    copy(TWIN, col_of(zz, xx, core), k).wait_send()
+                return 0
+
+            lax.fori_loop(0, PARTS, each, 0)
+
+            @pl.when(helper)
+            def _():
+                for xx in range(2):
+                    lent_copy(zz, xx).wait_send()
 
             return 0
 
-        lax.fori_loop(0, PARTS, each, 0)
-
-        @pl.when(helper)
-        def _():
-            for xx in range(2):
-                lent_copy(zz, xx).wait_send()
-
-        return 0
-
-    lax.fori_loop(0, line, drain, 0)
+        lax.fori_loop(0, line, drain, 0)
 
     def last(k, _):
-        @pl.when(to_up & (end | (k < SWAPPED)))
-        def _():
-            copy(UP, beside, k).wait_send()
-
-        @pl.when(to_down & (end | (k < SWAPPED)))
-        def _():
-            copy(DOWN, beside, k).wait_send()
-
         for step in range(1, rows):
 
             @pl.when(inner)

time: 51.1 us -> 49.7 us (0.973); the launches traced: 50.9 us -> 48.9 us
  Pallas kernels: 48.3 us -> 46.4 us
    pallas_call x1, Pallas kernels: 48.3 us -> 46.4 us  [on_device(): pl.pallas_call(functools.partial(body, rows, cols), out_shape=jax.ShapeDt...]
where the time goes in v3:
time: 49.7 us; the launch traced here: 48.9 us
  Pallas kernels  46.4 us (93%)
  local copies, waits for them, and re-layouts  2.55 us (5%)
    pallas_call x1, Pallas kernels, on_device(): pl.pallas_call(functools.partial(body, rows, cols), out_shape=jax.ShapeDt...  46.4 us
    unnamed x5, local copies, waits for them, and re-layouts  2.55 us

profile of v3, /device:TPU:0, one launch (start us, length us, event | category | flops | bytes accessed | tf_op | source)
XLA Modules:
  0.0 48.9 jit_solution(4425349195598237213)
XLA Ops:
  0.0 0.0 copy-start
  0.0 1.0 %copy-done = bf16[64,4000]{1,0:T(8,128)(2,1)S(1)} copy-done((bf16[64,4000]{1,0:T(8,128)(2,1)S(1)}, bf16[64,4000]{1,0:T(8,128)(2,1)}, u32[]{:S(2)}) %copy-start) | copy-done | bytes 512024
  1.0 0.0 copy-start.1
  1.0 0.7 %copy-done.1 = f32[4000]{0:T(1024)S(1)} copy-done((f32[4000]{0:T(1024)S(1)}, f32[4000]{0:T(1024)}, u32[]{:S(2)}) %copy-start.1) | copy-done | bytes 16024
  1.8 46.4 %shard_map.28 = f32[1024,128]{1,0:T(8,128)S(1)} custom-call(bf16[64,4000]{1,0:T(8,128)(2,1)S(1)} %copy-done, f32[1,4000]{1,0:T(1,128)S(1)} %bitcast.5), custom_call_target="tpu_custom_call" | custom-call | flops 1048576000 | bytes 1036288 | tf_op jit(solution)/shard_map/pallas_call | solution.py:353
  48.1 0.8 %copy.5 = f32[1024,1,128]{2,1,0:T(1,128)} copy(f32[1024,1,128]{2,1,0:T(1,128)S(1)} %bitcast.4) | data formatting | bytes 1048576
Async XLA Ops:
  0.0 1.0 %copy-start = (bf16[64,4000]{1,0:T(8,128)(2,1)S(1)}, bf16[64,4000]{1,0:T(8,128)(2,1)}, u32[]{:S(2)}) copy-start(bf16[64,4000]{1,0:T(8,128)(2,1)} %pair_ref.1) | copy-start | bytes 1536004
  1.0 0.7 %copy-start.1 = (f32[4000]{0:T(1024)S(1)}, f32[4000]{0:T(1024)}, u32[]{:S(2)}) copy-start(f32[4000]{0:T(1024)} %param.3) | copy-start | bytes 48004

commit v4 on v3

--- a/solution.py
+++ b/solution.py
@@ -8,8 +8,8 @@
 from jax.sharding import PartitionSpec as P
 
 UP, DOWN, SIDE, TWIN = range(4)
-PARTS = 4
-SWAPPED = 2
+PARTS = 2
+SWAPPED = 1
 LAG = 2
 
 

time: 49.7 us -> 47.9 us (0.964)
  Pallas kernels: 46.4 us -> 44.7 us
    pallas_call x1, Pallas kernels: 46.4 us -> 44.7 us  [on_device(): pl.pallas_call(functools.partial(body, rows, cols), out_shape=jax.ShapeDt...]
where the time goes in v4:
time: 47.9 us; the launch traced here: 47.3 us
  Pallas kernels  44.7 us (93%)
  local copies, waits for them, and re-layouts  2.55 us (5%)
    pallas_call x1, Pallas kernels, on_device(): pl.pallas_call(functools.partial(body, rows, cols), out_shape=jax.ShapeDt...  44.7 us
    unnamed x5, local copies, waits for them, and re-layouts  2.55 us

profile of v4, /device:TPU:0, one launch (start us, length us, event | category | flops | bytes accessed | tf_op | source)
XLA Modules:
  0.0 47.3 jit_solution(16833213539823212780)
XLA Ops:
  0.0 0.0 copy-start
  0.0 1.0 %copy-done = bf16[64,4000]{1,0:T(8,128)(2,1)S(1)} copy-done((bf16[64,4000]{1,0:T(8,128)(2,1)S(1)}, bf16[64,4000]{1,0:T(8,128)(2,1)}, u32[]{:S(2)}) %copy-start) | copy-done | bytes 512024
  1.0 0.0 copy-start.1
  1.0 0.7 %copy-done.1 = f32[4000]{0:T(1024)S(1)} copy-done((f32[4000]{0:T(1024)S(1)}, f32[4000]{0:T(1024)}, u32[]{:S(2)}) %copy-start.1) | copy-done | bytes 16024
  1.8 44.7 %shard_map.28 = f32[1024,128]{1,0:T(8,128)S(1)} custom-call(bf16[64,4000]{1,0:T(8,128)(2,1)S(1)} %copy-done, f32[1,4000]{1,0:T(1,128)S(1)} %bitcast.5), custom_call_target="tpu_custom_call" | custom-call | flops 1048576000 | bytes 1036288 | tf_op jit(solution)/shard_map/pallas_call | solution.py:353
  46.5 0.8 %copy.5 = f32[1024,1,128]{2,1,0:T(1,128)} copy(f32[1024,1,128]{2,1,0:T(1,128)S(1)} %bitcast.4) | data formatting | bytes 1048576
Async XLA Ops:
  0.0 1.0 %copy-start = (bf16[64,4000]{1,0:T(8,128)(2,1)S(1)}, bf16[64,4000]{1,0:T(8,128)(2,1)}, u32[]{:S(2)}) copy-start(bf16[64,4000]{1,0:T(8,128)(2,1)} %pair_ref.1) | copy-start | bytes 1536004
  1.0 0.7 %copy-start.1 = (f32[4000]{0:T(1024)S(1)}, f32[4000]{0:T(1024)}, u32[]{:S(2)}) copy-start(f32[4000]{0:T(1024)} %param.3) | copy-start | bytes 48004

commit v5 on v4

--- a/solution.py
+++ b/solution.py
@@ -124,7 +124,8 @@
         greet(device(DOWN))
 
     root = jnp.sqrt(weight_ref[...])
-    for k in range(PARTS):
+
+    def scale(k):
         here = pl.ds(k * part, part)
         value = (root * pair_ref[here].astype(jnp.float32)).astype(jnp.bfloat16)
         held[window(me, k)] = value
@@ -133,6 +134,7 @@
         def _():
             piece[window(my_row, k)] = value
 
+    scale(0)
     ends = (z == 0).astype(jnp.int32) + (z == line - 1).astype(jnp.int32)
     pl.semaphore_wait(barrier, 3 + rows - ends)
     beside = col_of(z, 1 - x, core)
@@ -227,7 +229,10 @@
 
         return 0
 
-    lax.fori_loop(0, ticks, advance, 0)
+    advance(jnp.int32(0), 0)
+    for k in range(1, PARTS):
+        scale(k)
+    lax.fori_loop(1, ticks, advance, 0)
 
     def row_wait(ward):
         def each(k, _):

time: 47.9 us -> 47.9 us (level)
  no operation moved by 1% of the time
where the time goes in v5:
time: 47.9 us; the launch traced here: 47.3 us
  Pallas kernels  44.7 us (93%)
  local copies, waits for them, and re-layouts  2.55 us (5%)
    pallas_call x1, Pallas kernels, on_device(): pl.pallas_call(functools.partial(body, rows, cols), out_shape=jax.ShapeDt...  44.7 us
    unnamed x5, local copies, waits for them, and re-layouts  2.55 us

profile of v5, /device:TPU:0, one launch (start us, length us, event | category | flops | bytes accessed | tf_op | source)
XLA Modules:
  0.0 47.3 jit_solution(5623396024228101926)
XLA Ops:
  0.0 0.0 copy-start
  0.0 1.0 %copy-done = bf16[64,4000]{1,0:T(8,128)(2,1)S(1)} copy-done((bf16[64,4000]{1,0:T(8,128)(2,1)S(1)}, bf16[64,4000]{1,0:T(8,128)(2,1)}, u32[]{:S(2)}) %copy-start) | copy-done | bytes 512024
  1.0 0.0 copy-start.1
  1.0 0.7 %copy-done.1 = f32[4000]{0:T(1024)S(1)} copy-done((f32[4000]{0:T(1024)S(1)}, f32[4000]{0:T(1024)}, u32[]{:S(2)}) %copy-start.1) | copy-done | bytes 16024
  1.8 44.7 %shard_map.28 = f32[1024,128]{1,0:T(8,128)S(1)} custom-call(bf16[64,4000]{1,0:T(8,128)(2,1)S(1)} %copy-done, f32[1,4000]{1,0:T(1,128)S(1)} %bitcast.5), custom_call_target="tpu_custom_call" | custom-call | flops 1048576000 | bytes 1036288 | tf_op jit(solution)/shard_map/pallas_call | solution.py:358
  46.5 0.8 %copy.5 = f32[1024,1,128]{2,1,0:T(1,128)} copy(f32[1024,1,128]{2,1,0:T(1,128)S(1)} %bitcast.4) | data formatting | bytes 1048576
Async XLA Ops:
  0.0 1.0 %copy-start = (bf16[64,4000]{1,0:T(8,128)(2,1)S(1)}, bf16[64,4000]{1,0:T(8,128)(2,1)}, u32[]{:S(2)}) copy-start(bf16[64,4000]{1,0:T(8,128)(2,1)} %pair_ref.1) | copy-start | bytes 1536004
  1.0 0.7 %copy-start.1 = (f32[4000]{0:T(1024)S(1)}, f32[4000]{0:T(1024)}, u32[]{:S(2)}) copy-start(f32[4000]{0:T(1024)} %param.3) | copy-start | bytes 48004
